TPU v7x, 32 devices: a whole 2x2x4 slice. The times are simulated.
32 devices in a mesh: grp: 4 (over x, core), blk: 8 (over z, y).
Axes of the slice: x: 2, y: 2, z: 4, core: 2. Of those that a mesh axis runs over, the one named last changes fastest.
Arguments:
- features: bfloat16 [4, 8, 4096, 256], P('grp', 'blk'), may hold values from -6 to 6
- hub_rows: int32 [4, 8, 32], P('grp', 'blk'), may hold values from 0 to 4095
- hub_adjacency: bfloat16 [4, 8, 4096, 256], P('grp', 'blk'), as said below
- tile_row: int32 [4, 8, 160], P('grp', 'blk'), may hold values from 0 to 31
- tile_col: int32 [4, 8, 160], P('grp', 'blk'), may hold values from 0 to 39
- tile_count: int32 [4, 8], P('grp', 'blk'), may hold values from 26 to 160, as said below
- tile_values: bfloat16 [4, 8, 160, 128, 128], P('grp', 'blk'), may hold values from 0 to 0.049804688
- send_rows: int32 [4, 8, 4, 8, 32], P('grp', 'blk'), may hold values from 0 to 4095
- weight: bfloat16 [256, 256], replicated, may hold values from -0.375 to 0.375
Outputs:
- activations: bfloat16 [4, 8, 4096, 256], P('grp', 'blk')
Inputs may be any that keep to these rules, and one draw needn't show every extreme that they name: `tile_count`: some device has exactly 160 live tile slots in every draw. `hub_adjacency`: Non-negative edge weights.
All inputs are finite; a program needn't handle non-finite values.
Results may differ from a plain program's by a relative error of at most 0.0014.
The roundings to bfloat16 on the way count: a program that leaves them out, or rounds other values in their place, can miss the bound.
Values may be sent and summed in bfloat16 or wider, within the bound.
A program may use at most 128 MiB of HBM per device.

v0:
```python
import functools

import jax
import jax.numpy as jnp
from jax import lax
from jax.experimental import pallas as pl
from jax.experimental.pallas import tpu as pltpu
from jax.sharding import PartitionSpec as P

TB = 128
MESH = pl.DeviceIdType.MESH
ANY = pl.BlockSpec(memory_space=pl.ANY)
VMEM = pl.BlockSpec(memory_space=pltpu.VMEM)
SMEM = pl.BlockSpec(memory_space=pltpu.SMEM)

PART = 16
GROUP = 4
CHUNK = 512


def pick(listing, feats):
    lists, entries = listing.shape
    blocks, _, width = feats.shape
    count = lists * entries
    wide = jnp.broadcast_to(listing[:, :, None], (lists, entries, CHUNK)).reshape(count, CHUNK)
    offset = wide - lax.broadcasted_iota(jnp.int32, (count, CHUNK), 1)
    total = jnp.zeros((count, width), jnp.float32)
    step = CHUNK // TB
    for at in range(0, blocks, step):
        chosen = jnp.where(offset == at * TB, 1.0, 0.0).astype(jnp.bfloat16)
        part = feats[at : at + step].reshape(CHUNK, width)
        total += jnp.dot(chosen, part, preferred_element_type=jnp.float32)
    return total.astype(jnp.bfloat16)


def exchange_kernel(
    groups, blocks, count_ref, feats_hbm, hub_rows_hbm, send_rows_hbm, adj_hbm, row_hbm, col_hbm, tiles_hbm,
    received_ref, partial_hbm,
    feats, hub_rows, send_rows, adj, row_list, col_list, col_at, tiles, links, last, link_at, last_at,
    stage, hub, steps, partial,
    in_sem, tile_sem, link_sem, out_sem, own_sem,
    send_sem, recv_sem, far_send, far_recv, near_send, near_recv,
):
    g = lax.axis_index("grp")
    b = lax.axis_index("blk")
    entries = send_rows.shape[2]
    hub_dev = hub.shape[1]
    row_blocks, _, width = feats.shape
    slots = tiles.shape[0]
    half = blocks // 2
    me = g * blocks + b
    devices = groups * blocks
    high = b // 2
    low = lax.rem(b, 2)

    barrier = pltpu.get_barrier_semaphore()

    def greet(off, _):
        other = lax.rem(me + off, devices)
        pl.semaphore_signal(
            barrier, inc=1, device_id=(other // blocks, lax.rem(other, blocks)), device_id_type=MESH
        )
        return 0

    ins = [
        pltpu.make_async_copy(hub_rows_hbm, hub_rows, in_sem.at[0]),
        pltpu.make_async_copy(send_rows_hbm, send_rows, in_sem.at[1]),
        pltpu.make_async_copy(feats_hbm, feats, in_sem.at[2]),
        pltpu.make_async_copy(row_hbm, row_list, in_sem.at[3]),
        pltpu.make_async_copy(col_hbm, col_list, in_sem.at[4]),
        pltpu.make_async_copy(col_hbm, col_at, in_sem.at[5]),
        pltpu.make_async_copy(adj_hbm, adj, in_sem.at[6]),
    ]

    def tile_copy(c):
        at = pl.ds(c * PART, PART)
        return pltpu.make_async_copy(tiles_hbm.at[at], tiles.at[at], tile_sem.at[c])

    for copy in ins[:6]:
        copy.start()
    lax.fori_loop(1, devices, greet, 0)
    for copy in ins[:3]:
        copy.wait()

    def boundary_copy(j, k, dst_g, dst_b, slot):
        return pltpu.make_async_remote_copy(
            src_ref=stage.at[dst_g * blocks + dst_b],
            dst_ref=received_ref.at[slot],
            send_sem=send_sem.at[j, k],
            recv_sem=recv_sem.at[j, k],
            device_id=(dst_g, dst_b),
            device_id_type=MESH,
        )

    def far_high(k):
        return lax.rem(high + half - k, half)

    def far_copy(k, block):
        return pltpu.make_async_remote_copy(
            src_ref=hub.at[block],
            dst_ref=hub.at[block],
            send_sem=far_send.at[k],
            recv_sem=far_recv.at[k],
            device_id=(g, lax.rem(high + k, half) * 2 + low),
            device_id_type=MESH,
        )

    def near_copy(k, block):
        return pltpu.make_async_remote_copy(
            src_ref=hub.at[block],
            dst_ref=hub.at[block],
            send_sem=near_send.at[k],
            recv_sem=near_recv.at[k],
            device_id=(g, high * 2 + 1 - low),
            device_id_type=MESH,
        )

    def place(dst_g, rows):
        stage[pl.ds(dst_g * blocks, blocks)] = rows.reshape(blocks, entries, width)

    def send(j, dst_g):
        def one(k, _):
            dst_b = lax.rem(b + half + k, blocks)

            @pl.when((dst_g != g) | (dst_b != b))
            def _():
                boundary_copy(j, k, dst_g, dst_b, me).start()

            return 0

        lax.fori_loop(0, blocks, one, 0)

    def chunk(j, _):
        dst_g = lax.rem(g + j, groups)
        place(dst_g, pick(send_rows[dst_g], feats))
        send(j, dst_g)
        return 0

    first_g = lax.rem(g + 1, groups)
    rows = pick(jnp.concatenate([send_rows[first_g], hub_rows[...]], 0), feats)
    place(first_g, rows[: blocks * entries])
    hub[b] = rows[blocks * entries :]
    pl.semaphore_wait(barrier, devices - 1)
    for k in range(1, half):
        far_copy(k, b).start()
    near_copy(0, b).start()
    send(1, first_g)
    ins[6].start()
    for c in range(slots // PART):
        tile_copy(c).start()
    lax.fori_loop(2, groups, chunk, 0)
    chunk(0, 0)
    own = pltpu.make_async_copy(stage.at[me], received_ref.at[me], own_sem)
    own.start()

    for copy in ins[3:6]:
        copy.wait()
    live = (lax.broadcasted_iota(jnp.int32, (1, slots), 1) < count_ref[0]) & (col_list[...] < row_blocks)
    key = jnp.where(live, row_list[...], -1)
    key = jnp.broadcast_to(key[:, :, None], (1, slots, slots)).reshape(slots, slots)
    slot = lax.broadcasted_iota(jnp.int32, (slots, slots), 0)
    place_at = lax.broadcasted_iota(jnp.int32, (slots, slots), 1)

    def latest(hit):
        found = jnp.max(jnp.where(hit, slot, -1), axis=0, keepdims=True)
        return jnp.where(found < 0, slots, found)

    links[...] = latest((key == row_list[...]) & (slot < place_at))
    last[...] = latest(key == place_at)
    to_smem = [
        pltpu.make_async_copy(links, link_at, link_sem.at[0]),
        pltpu.make_async_copy(last, last_at, link_sem.at[1]),
    ]
    for copy in to_smem:
        copy.start()

    for k in range(1, half):
        block = far_high(k) * 2 + low
        far_copy(k, block).wait_recv()
        near_copy(k, block).start()

    steps[slots] = jnp.zeros((TB, width), jnp.float32)
    for copy in to_smem:
        copy.wait()

    def part(c, _):
        tile_copy(c).wait()

        def group(u, _):
            products = []
            for i in range(GROUP):
                t = c * PART + u * GROUP + i
                block = feats[jnp.clip(col_at[0, t], 0, row_blocks - 1)]
                products.append(jnp.dot(tiles[t], block, preferred_element_type=jnp.float32))
            for i in range(GROUP):
                t = c * PART + u * GROUP + i
                steps[t] = steps[jnp.clip(link_at[0, t], 0, slots)] + products[i]
            return 0

        return lax.fori_loop(0, PART // GROUP, group, 0)

    lax.fori_loop(0, slots // PART, part, 0)

    ins[6].wait()
    for k in range(half):
        near_copy(k, far_high(k) * 2 + 1 - low).wait_recv()

    def out_copy(i):
        return pltpu.make_async_copy(partial.at[i], partial_hbm.at[i], out_sem.at[i])

    hub_all = hub[...].reshape(blocks * hub_dev, width)
    per = CHUNK // TB

    def finish_rows(i, _):
        summed = jnp.dot(adj[i], hub_all, preferred_element_type=jnp.float32)
        for r in range(per):
            partial[i, r * TB : (r + 1) * TB] = (
                summed[r * TB : (r + 1) * TB] + steps[jnp.clip(last_at[0, i * per + r], 0, slots)]
            )
        out_copy(i).start()
        return 0

    lax.fori_loop(0, row_blocks // per, finish_rows, 0)

    for k in range(1, half):
        far_copy(k, b).wait_send()
    for k in range(half):
        near_copy(k, far_high(k) * 2 + low).wait_send()

    def finish(at, _):
        j = at // blocks
        k = lax.rem(at, blocks)
        src_g = lax.rem(g + groups - j, groups)
        src_b = lax.rem(b + 2 * blocks - half - k, blocks)

        @pl.when((src_g != g) | (src_b != b))
        def _():
            arrived = boundary_copy(
                j, k, lax.rem(g + j, groups), lax.rem(b + half + k, blocks), src_g * blocks + src_b
            )
            arrived.wait_send()
            arrived.wait_recv()

        return 0

    lax.fori_loop(0, devices, finish, 0)
    own.wait()

    def drain(i, _):
        out_copy(i).wait()
        return 0

    lax.fori_loop(0, row_blocks // per, drain, 0)


def layer_kernel(
    count_ref, row_ref, col_ref, received_hbm, partial_hbm, tiles_hbm, weight_hbm,
    out_hbm,
    received, tiles, weight, total, result, picked, in_sem, part_sem, tile_sem, out_sem,
):
    row_blocks = total.shape[0] - 1
    per = CHUNK // TB
    chunks = row_blocks // per
    live = count_ref[0]

    ins = [
        pltpu.make_async_copy(received_hbm, received, in_sem.at[0]),
        pltpu.make_async_copy(weight_hbm, weight, in_sem.at[1]),
    ]

    def part_copy(i):
        at = pl.ds(i * per, per)
        return pltpu.make_async_copy(partial_hbm.at[at], total.at[at], part_sem.at[i])

    for copy in ins:
        copy.start()

    def tile_copy(t, n):
        return pltpu.make_async_copy(tiles_hbm.at[t], tiles.at[n], tile_sem.at[n])

    def collect(t, n):
        remote = col_ref[t] >= row_blocks

        @pl.when(remote)
        def _():
            picked[n] = t
            tile_copy(t, n).start()

        return n + remote.astype(jnp.int32)

    for i in range(chunks):
        part_copy(i).start()
    number = lax.fori_loop(0, live, collect, 0)
    for copy in ins:
        copy.wait()
    for i in range(chunks):
        part_copy(i).wait()

    @pl.loop(0, (number + GROUP - 1) // GROUP)
    def _(u):
        for i in range(GROUP):
            n = u * GROUP + i

            @pl.when(n < number)
            def _():
                tile_copy(picked[n], n).wait()

        products = []
        places = []
        for i in range(GROUP):
            n = u * GROUP + i
            t = picked[jnp.minimum(n, number - 1)]
            block = received[col_ref[t] - row_blocks]
            products.append(jnp.dot(tiles[n], block, preferred_element_type=jnp.float32))
            places.append(jnp.where(n < number, row_ref[t], row_blocks))
        for product, place in zip(products, places):
            total[place] += product

    def out_copy(i):
        at = pl.ds(i * CHUNK, CHUNK)
        return pltpu.make_async_copy(result.at[at], out_hbm.at[at], out_sem.at[i])

    for i in range(chunks):
        rows = total[i * per : (i + 1) * per].reshape(CHUNK, total.shape[2])
        mixed = jnp.dot(rows.astype(jnp.bfloat16), weight[...], preferred_element_type=jnp.float32)
        result[i * CHUNK : (i + 1) * CHUNK, :] = jnp.maximum(mixed, 0.0).astype(jnp.bfloat16)
        out_copy(i).start()
    for i in range(chunks):
        out_copy(i).wait()


def per_device(
    groups, blocks, features, hub_rows, hub_adjacency, tile_row, tile_col, tile_count,
    tile_values, send_rows, weight,
):
    local = features[0, 0]
    rows, width = local.shape
    entries = send_rows.shape[-1]
    hub_dev = hub_rows.shape[-1]
    hubs = blocks * hub_dev
    devices = groups * blocks
    slots = tile_row.shape[-1]
    row_blocks = rows // TB
    chunks = rows // CHUNK
    half = blocks // 2
    bf16 = jnp.bfloat16
    f32 = jnp.float32
    i32 = jnp.int32
    dma = pltpu.SemaphoreType.DMA
    received, partial = pl.pallas_call(
        functools.partial(exchange_kernel, groups, blocks),
        out_shape=(
            jax.ShapeDtypeStruct((devices, entries, width), bf16),
            jax.ShapeDtypeStruct((chunks, CHUNK, width), f32),
        ),
        in_specs=[SMEM] + [ANY] * 7,
        out_specs=(ANY, ANY),
        scratch_shapes=[
            pltpu.VMEM((row_blocks, TB, width), bf16),
            pltpu.VMEM((1, hub_dev), i32),
            pltpu.VMEM((groups, blocks, entries), i32),
            pltpu.VMEM((chunks, CHUNK, hubs), bf16),
            pltpu.VMEM((1, slots), i32),
            pltpu.VMEM((1, slots), i32),
            pltpu.SMEM((1, slots), i32),
            pltpu.VMEM((slots, TB, TB), bf16),
            pltpu.VMEM((1, slots), i32),
            pltpu.VMEM((1, slots), i32),
            pltpu.SMEM((1, slots), i32),
            pltpu.SMEM((1, slots), i32),
            pltpu.VMEM((devices, entries, width), bf16),
            pltpu.VMEM((blocks, hub_dev, width), bf16),
            pltpu.VMEM((slots + 1, TB, width), f32),
            pltpu.VMEM((chunks, CHUNK, width), f32),
            dma((7,)),
            dma((slots // PART,)),
            dma((2,)),
            dma((chunks,)),
            dma(()),
            dma((groups, blocks)),
            dma((groups, blocks)),
            dma((half,)),
            dma((half,)),
            dma((half,)),
            dma((half,)),
        ],
        compiler_params=pltpu.CompilerParams(
            collective_id=0, has_side_effects=True, vmem_limit_bytes=60 << 20
        ),
        name="exchange",
    )(
        tile_count[0], local.reshape(row_blocks, TB, width), hub_rows[0], send_rows[0, 0],
        hub_adjacency[0, 0].reshape(chunks, CHUNK, hubs), tile_row[0], tile_col[0], tile_values[0, 0],
    )
    out = pl.pallas_call(
        layer_kernel,
        out_shape=jax.ShapeDtypeStruct((rows, width), bf16),
        in_specs=[SMEM, SMEM, SMEM, ANY, ANY, ANY, ANY],
        out_specs=ANY,
        scratch_shapes=[
            pltpu.VMEM((devices * entries // TB, TB, width), bf16),
            pltpu.VMEM((slots, TB, TB), bf16),
            pltpu.VMEM(weight.shape, bf16),
            pltpu.VMEM((row_blocks + 1, TB, width), f32),
            pltpu.VMEM((rows, width), bf16),
            pltpu.SMEM((slots,), i32),
            dma((2,)),
            dma((chunks,)),
            dma((slots,)),
            dma((chunks,)),
        ],
        compiler_params=pltpu.CompilerParams(vmem_limit_bytes=60 << 20),
        name="layer",
    )(
        tile_count[0], tile_row[0, 0], tile_col[0, 0],
        received.reshape(devices * entries // TB, TB, width),
        partial.reshape(row_blocks, TB, width), tile_values[0, 0], weight,
    )
    return out[None, None]


def solution(mesh):
    return jax.shard_map(
        functools.partial(per_device, mesh.shape["grp"], mesh.shape["blk"]),
        mesh=mesh,
        in_specs=(
            P("grp", "blk", None, None),
            P("grp", "blk", None),
            P("grp", "blk", None, None),
            P("grp", "blk", None),
            P("grp", "blk", None),
            P("grp", "blk"),
            P("grp", "blk", None, None, None),
            P("grp", "blk", None, None, None),
            P(),
        ),
        out_specs=P("grp", "blk", None, None),
        check_vma=False,
    )
```

profile of v0, /device:TPU:0, one launch (start us, length us, event | category | flops | bytes accessed | tf_op | source)
XLA Modules:
  0.0 31.8 jit_solution(10772128983986121213)
XLA Ops:
  0.7 23.7 %exchange.1 = (bf16[32,32,256]{2,1,0:T(8,128)(2,1)}, f32[8,512,256]{2,1,0:T(8,128)}) custom-call(s32[1]{0:T(128)} %bitcast.13.count_ref, bf16[32,128,256]{2,1,0:T(8,128)(2,1)} %bitcast.18, s32[1,32]{1,0:T(1,128)} %bitcast.26, s32[4,8,32]{2,1,0:T(8,128)} %bitcast.21, bf16[8,512,256]{2,1,0:T(8,128)(2,1)} %bitcast.19, s32[1,160]{1,0:T(1,128)} %bitcast.22, ...), custom_call_target="tpu_custom_call" | custom-call | tf_op jit(solution)/shard_map/exchange/pallas_call | solution.py:350
  24.4 7.4 %layer.1 = bf16[4096,256]{1,0:T(8,128)(2,1)} custom-call(s32[1]{0:T(128)} %bitcast.14.count_ref, s32[160]{0:T(256)} %bitcast.23, s32[160]{0:T(256)} %bitcast.25, bf16[8,128,256]{2,1,0:T(8,128)(2,1)} %bitcast.20, f32[32,128,256]{2,1,0:T(8,128)} %bitcast.17, bf16[160,128,128]{2,1,0:T(8,128)(2,1)} %bitcast.16, bf16[256,256]{1,0:T(8,128)(2,1)} %weight_hbm.1), custom_call_target="tpu_custom_call" | custom-call | tf_op jit(solution)/shard_map/layer/pallas_call | solution.py:395
where the time goes:
time: 32.4 us; the launch traced here: 31.8 us
  Pallas kernels  31.2 us (96%)
  between operations  0.66 us (2%)
    pallas_call x1, Pallas kernels, per_device(): pl.pallas_call(functools.partial(exchange_kernel, groups, blocks), out_sh...  23.7 us
    pallas_call x1, Pallas kernels, per_device(): pl.pallas_call(layer_kernel, out_shape=jax.ShapeDtypeStruct((rows, width)...  7.44 us

commit v1 on v0

--- a/solution.py
+++ b/solution.py
@@ -18,7 +18,7 @@
 CHUNK = 512
 
 
-def pick(listing, feats):
+def pick(listing, feats, arrive=None):
     lists, entries = listing.shape
     blocks, _, width = feats.shape
     count = lists * entries
@@ -27,6 +27,8 @@
     total = jnp.zeros((count, width), jnp.float32)
     step = CHUNK // TB
     for at in range(0, blocks, step):
+        if arrive is not None:
+            arrive(at)
         chosen = jnp.where(offset == at * TB, 1.0, 0.0).astype(jnp.bfloat16)
         part = feats[at : at + step].reshape(CHUNK, width)
         total += jnp.dot(chosen, part, preferred_element_type=jnp.float32)
@@ -36,9 +38,10 @@
 def exchange_kernel(
     groups, blocks, count_ref, feats_hbm, hub_rows_hbm, send_rows_hbm, adj_hbm, row_hbm, col_hbm, tiles_hbm,
     received_ref, partial_hbm,
-    feats, hub_rows, send_rows, adj, row_list, col_list, col_at, tiles, links, last, link_at, last_at,
+    feats, hub_rows, send_rows, adj, row_list, col_list, col_at, tiles,
+    links, last, firsts, seconds, link_at, last_at, first_at, second_at,
     stage, hub, steps, partial,
-    in_sem, tile_sem, link_sem, out_sem, own_sem,
+    in_sem, feats_sem, tile_sem, link_sem, out_sem, own_sem,
     send_sem, recv_sem, far_send, far_recv, near_send, near_recv,
 ):
     g = lax.axis_index("grp")
@@ -46,7 +49,7 @@
     entries = send_rows.shape[2]
     hub_dev = hub.shape[1]
     row_blocks, _, width = feats.shape
-    slots = tiles.shape[0]
+    slots = row_list.shape[1]
     half = blocks // 2
     me = g * blocks + b
     devices = groups * blocks
@@ -65,21 +68,34 @@
     ins = [
         pltpu.make_async_copy(hub_rows_hbm, hub_rows, in_sem.at[0]),
         pltpu.make_async_copy(send_rows_hbm, send_rows, in_sem.at[1]),
-        pltpu.make_async_copy(feats_hbm, feats, in_sem.at[2]),
-        pltpu.make_async_copy(row_hbm, row_list, in_sem.at[3]),
-        pltpu.make_async_copy(col_hbm, col_list, in_sem.at[4]),
-        pltpu.make_async_copy(col_hbm, col_at, in_sem.at[5]),
-        pltpu.make_async_copy(adj_hbm, adj, in_sem.at[6]),
+        pltpu.make_async_copy(row_hbm, row_list, in_sem.at[2]),
+        pltpu.make_async_copy(col_hbm, col_list, in_sem.at[3]),
+        pltpu.make_async_copy(col_hbm, col_at, in_sem.at[4]),
+        pltpu.make_async_copy(adj_hbm, adj, in_sem.at[5]),
     ]
 
     def tile_copy(c):
         at = pl.ds(c * PART, PART)
         return pltpu.make_async_copy(tiles_hbm.at[at], tiles.at[at], tile_sem.at[c])
 
-    for copy in ins[:6]:
+    quarter = row_blocks // 4
+
+    def feats_copy(i):
+        at = pl.ds(i * quarter, quarter)
+        return pltpu.make_async_copy(feats_hbm.at[at], feats.at[at], feats_sem.at[i])
+
+    def arrive(at):
+        if at % quarter == 0:
+            feats_copy(at // quarter).wait()
+
+    for copy in ins[:2]:
+        copy.start()
+    for i in range(4):
+        feats_copy(i).start()
+    for copy in ins[2:5]:
         copy.start()
     lax.fori_loop(1, devices, greet, 0)
-    for copy in ins[:3]:
+    for copy in ins[:2]:
         copy.wait()
 
     def boundary_copy(j, k, dst_g, dst_b, slot):
@@ -137,7 +153,7 @@
         return 0
 
     first_g = lax.rem(g + 1, groups)
-    rows = pick(jnp.concatenate([send_rows[first_g], hub_rows[...]], 0), feats)
+    rows = pick(jnp.concatenate([send_rows[first_g], hub_rows[...]], 0), feats, arrive)
     place(first_g, rows[: blocks * entries])
     hub[b] = rows[blocks * entries :]
     pl.semaphore_wait(barrier, devices - 1)
@@ -145,7 +161,7 @@
         far_copy(k, b).start()
     near_copy(0, b).start()
     send(1, first_g)
-    ins[6].start()
+    ins[5].start()
     for c in range(slots // PART):
         tile_copy(c).start()
     lax.fori_loop(2, groups, chunk, 0)
@@ -153,23 +169,44 @@
     own = pltpu.make_async_copy(stage.at[me], received_ref.at[me], own_sem)
     own.start()
 
-    for copy in ins[3:6]:
+    for copy in ins[2:5]:
         copy.wait()
+    pairs = link_at.shape[1]
     live = (lax.broadcasted_iota(jnp.int32, (1, slots), 1) < count_ref[0]) & (col_list[...] < row_blocks)
-    key = jnp.where(live, row_list[...], -1)
-    key = jnp.broadcast_to(key[:, :, None], (1, slots, slots)).reshape(slots, slots)
-    slot = lax.broadcasted_iota(jnp.int32, (slots, slots), 0)
-    place_at = lax.broadcasted_iota(jnp.int32, (slots, slots), 1)
-
-    def latest(hit):
-        found = jnp.max(jnp.where(hit, slot, -1), axis=0, keepdims=True)
-        return jnp.where(found < 0, slots, found)
-
-    links[...] = latest((key == row_list[...]) & (slot < place_at))
-    last[...] = latest(key == place_at)
+    key = jnp.where(live, row_list[...], row_blocks)
+    key_down = jnp.broadcast_to(key[:, :, None], (1, slots, slots)).reshape(slots, slots)
+    down = lax.broadcasted_iota(jnp.int32, (slots, slots), 0)
+    across = lax.broadcasted_iota(jnp.int32, (slots, slots), 1)
+
+    def tally(hit, axis):
+        return jnp.sum(jnp.where(hit, 1, 0), axis=axis, keepdims=True)
+
+    same = key_down == key
+    rank_across = tally(same & (down < across), 0)
+    rank_down = tally(same & (across < down), 1)
+    opens = lax.rem(rank_across, 2) == 0
+    before = tally((key < key_down) & opens, 1)
+    code = jnp.where(key_down[:, :1] < row_blocks, 2 * before + rank_down, -1)
+
+    def pick_slot(which, value, none):
+        found = jnp.max(jnp.where(which, value, -1), axis=0, keepdims=True)
+        return jnp.where(found < 0, none, found)
+
+    wanted = 2 * lax.broadcasted_iota(jnp.int32, (slots, pairs), 1)
+    slot = lax.broadcasted_iota(jnp.int32, (slots, pairs), 0)
+    code = jnp.broadcast_to(code, (slots, pairs))
+    firsts[...] = pick_slot(code == wanted, slot, slots)
+    seconds[...] = pick_slot(code == wanted + 1, slot, slots)
+    rank_wide = jnp.broadcast_to(rank_down, (slots, pairs))
+    links[...] = pick_slot((code == wanted) & (rank_wide > 0), wanted // 2 - 1, pairs)
+    row_at = lax.broadcasted_iota(jnp.int32, (slots, pairs), 1)
+    key_wide = jnp.broadcast_to(key[:, :, None], (1, slots, pairs)).reshape(slots, pairs)
+    last[...] = pick_slot(key_wide == row_at, code // 2, pairs)
     to_smem = [
         pltpu.make_async_copy(links, link_at, link_sem.at[0]),
         pltpu.make_async_copy(last, last_at, link_sem.at[1]),
+        pltpu.make_async_copy(firsts, first_at, link_sem.at[2]),
+        pltpu.make_async_copy(seconds, second_at, link_sem.at[3]),
     ]
     for copy in to_smem:
         copy.start()
@@ -179,29 +216,33 @@
         far_copy(k, block).wait_recv()
         near_copy(k, block).start()
 
-    steps[slots] = jnp.zeros((TB, width), jnp.float32)
+    steps[pairs] = jnp.zeros((TB, width), jnp.float32)
+    tiles[slots] = jnp.zeros((TB, TB), tiles.dtype)
     for copy in to_smem:
         copy.wait()
-
-    def part(c, _):
+    for c in range(slots // PART):
         tile_copy(c).wait()
 
-        def group(u, _):
-            products = []
-            for i in range(GROUP):
-                t = c * PART + u * GROUP + i
-                block = feats[jnp.clip(col_at[0, t], 0, row_blocks - 1)]
-                products.append(jnp.dot(tiles[t], block, preferred_element_type=jnp.float32))
-            for i in range(GROUP):
-                t = c * PART + u * GROUP + i
-                steps[t] = steps[jnp.clip(link_at[0, t], 0, slots)] + products[i]
-            return 0
-
-        return lax.fori_loop(0, PART // GROUP, group, 0)
-
-    lax.fori_loop(0, slots // PART, part, 0)
-
-    ins[6].wait()
+    def slot_block(t):
+        return feats[jnp.clip(col_at[0, jnp.clip(t, 0, slots - 1)], 0, row_blocks - 1)]
+
+    def group(u, _):
+        products = []
+        for i in range(GROUP):
+            n = u * GROUP + i
+            one = jnp.clip(first_at[0, n], 0, slots)
+            two = jnp.clip(second_at[0, n], 0, slots)
+            weights = jnp.concatenate([tiles[one], tiles[two]], 1)
+            blocks_in = jnp.concatenate([slot_block(one), slot_block(two)], 0)
+            products.append(jnp.dot(weights, blocks_in, preferred_element_type=jnp.float32))
+        for i in range(GROUP):
+            n = u * GROUP + i
+            steps[n] = steps[jnp.clip(link_at[0, n], 0, pairs)] + products[i]
+        return 0
+
+    lax.fori_loop(0, pairs // GROUP, group, 0)
+
+    ins[5].wait()
     for k in range(half):
         near_copy(k, far_high(k) * 2 + 1 - low).wait_recv()
 
@@ -215,7 +256,7 @@
         summed = jnp.dot(adj[i], hub_all, preferred_element_type=jnp.float32)
         for r in range(per):
             partial[i, r * TB : (r + 1) * TB] = (
-                summed[r * TB : (r + 1) * TB] + steps[jnp.clip(last_at[0, i * per + r], 0, slots)]
+                summed[r * TB : (r + 1) * TB] + steps[jnp.clip(last_at[0, i * per + r], 0, pairs)]
             )
         out_copy(i).start()
         return 0
@@ -343,6 +384,7 @@
     row_blocks = rows // TB
     chunks = rows // CHUNK
     half = blocks // 2
+    pairs = -(-(slots + row_blocks) // (2 * GROUP)) * GROUP
     bf16 = jnp.bfloat16
     f32 = jnp.float32
     i32 = jnp.int32
@@ -363,18 +405,23 @@
             pltpu.VMEM((1, slots), i32),
             pltpu.VMEM((1, slots), i32),
             pltpu.SMEM((1, slots), i32),
-            pltpu.VMEM((slots, TB, TB), bf16),
-            pltpu.VMEM((1, slots), i32),
-            pltpu.VMEM((1, slots), i32),
-            pltpu.SMEM((1, slots), i32),
-            pltpu.SMEM((1, slots), i32),
+            pltpu.VMEM((slots + 1, TB, TB), bf16),
+            pltpu.VMEM((1, pairs), i32),
+            pltpu.VMEM((1, pairs), i32),
+            pltpu.VMEM((1, pairs), i32),
+            pltpu.VMEM((1, pairs), i32),
+            pltpu.SMEM((1, pairs), i32),
+            pltpu.SMEM((1, pairs), i32),
+            pltpu.SMEM((1, pairs), i32),
+            pltpu.SMEM((1, pairs), i32),
             pltpu.VMEM((devices, entries, width), bf16),
             pltpu.VMEM((blocks, hub_dev, width), bf16),
-            pltpu.VMEM((slots + 1, TB, width), f32),
+            pltpu.VMEM((pairs + 1, TB, width), f32),
             pltpu.VMEM((chunks, CHUNK, width), f32),
-            dma((7,)),
+            dma((6,)),
+            dma((4,)),
             dma((slots // PART,)),
-            dma((2,)),
+            dma((4,)),
             dma((chunks,)),
             dma(()),
             dma((groups, blocks)),

time: 32.4 us -> 31.3 us (0.966)
  Pallas kernels: 31.2 us -> 30.1 us
    pallas_call x1, Pallas kernels: 23.7 us -> 23.1 us  [per_device(): pl.pallas_call(functools.partial(exchange_kernel, groups, blocks), out_sh...]
    pallas_call x1, Pallas kernels: 7.44 us -> 6.96 us  [per_device(): pl.pallas_call(layer_kernel, out_shape=jax.ShapeDtypeStruct((rows, width)...]
where the time goes in v1:
time: 31.3 us; the launch traced here: 30.7 us
  Pallas kernels  30.1 us (96%)
  between operations  0.66 us (2%)
    pallas_call x1, Pallas kernels, per_device(): pl.pallas_call(functools.partial(exchange_kernel, groups, blocks), out_sh...  23.1 us
    pallas_call x1, Pallas kernels, per_device(): pl.pallas_call(layer_kernel, out_shape=jax.ShapeDtypeStruct((rows, width)...  6.96 us

profile of v1, /device:TPU:0, one launch (start us, length us, event | category | flops | bytes accessed | tf_op | source)
XLA Modules:
  0.0 30.7 jit_solution(7594938841192266919)
XLA Ops:
  0.7 23.1 %exchange.1 = (bf16[32,32,256]{2,1,0:T(8,128)(2,1)}, f32[8,512,256]{2,1,0:T(8,128)}) custom-call(s32[1]{0:T(128)} %bitcast.13.count_ref, bf16[32,128,256]{2,1,0:T(8,128)(2,1)} %bitcast.18, s32[1,32]{1,0:T(1,128)} %bitcast.26, s32[4,8,32]{2,1,0:T(8,128)} %bitcast.21, bf16[8,512,256]{2,1,0:T(8,128)(2,1)} %bitcast.19, s32[1,160]{1,0:T(1,128)} %bitcast.22, ...), custom_call_target="tpu_custom_call" | custom-call | tf_op jit(solution)/shard_map/exchange/pallas_call | solution.py:392
  23.8 7.0 %layer.1 = bf16[4096,256]{1,0:T(8,128)(2,1)} custom-call(s32[1]{0:T(128)} %bitcast.14.count_ref, s32[160]{0:T(256)} %bitcast.23, s32[160]{0:T(256)} %bitcast.25, bf16[8,128,256]{2,1,0:T(8,128)(2,1)} %bitcast.20, f32[32,128,256]{2,1,0:T(8,128)} %bitcast.17, bf16[160,128,128]{2,1,0:T(8,128)(2,1)} %bitcast.16, bf16[256,256]{1,0:T(8,128)(2,1)} %weight_hbm.1), custom_call_target="tpu_custom_call" | custom-call | tf_op jit(solution)/shard_map/layer/pallas_call | solution.py:442

commit v2 on v1

--- a/solution.py
+++ b/solution.py
@@ -37,11 +37,11 @@
 
 def exchange_kernel(
     groups, blocks, count_ref, feats_hbm, hub_rows_hbm, send_rows_hbm, adj_hbm, row_hbm, col_hbm, tiles_hbm,
-    received_ref, partial_hbm,
+    received_ref, partial_hbm, plan_hbm,
     feats, hub_rows, send_rows, adj, row_list, col_list, col_at, tiles,
     links, last, firsts, seconds, link_at, last_at, first_at, second_at,
-    stage, hub, steps, partial,
-    in_sem, feats_sem, tile_sem, link_sem, out_sem, own_sem,
+    stage, hub, steps, partial, plan,
+    in_sem, feats_sem, tile_sem, link_sem, out_sem, own_sem, plan_sem,
     send_sem, recv_sem, far_send, far_recv, near_send, near_recv,
 ):
     g = lax.axis_index("grp")
@@ -136,11 +136,12 @@
 
     def send(j, dst_g):
         def one(k, _):
-            dst_b = lax.rem(b + half + k, blocks)
+            off = (1 - lax.rem(k + g, 2)) * half + k // 2
+            dst_b = lax.rem(b + off, blocks)
 
             @pl.when((dst_g != g) | (dst_b != b))
             def _():
-                boundary_copy(j, k, dst_g, dst_b, me).start()
+                boundary_copy(j, off, dst_g, dst_b, me).start()
 
             return 0
 
@@ -202,6 +203,22 @@
     row_at = lax.broadcasted_iota(jnp.int32, (slots, pairs), 1)
     key_wide = jnp.broadcast_to(key[:, :, None], (1, slots, pairs)).reshape(slots, pairs)
     last[...] = pick_slot(key_wide == row_at, code // 2, pairs)
+
+    far = (lax.broadcasted_iota(jnp.int32, (1, slots), 1) < count_ref[0]) & (col_list[...] >= row_blocks)
+    far_key = jnp.where(far, row_list[...], row_blocks)
+
+    def column(values):
+        return jnp.broadcast_to(values[:, :, None], (1, slots, slots)).reshape(slots, slots)
+
+    far_down = column(far_key)
+    position = tally((far_key < far_down) | ((far_key == far_down) & (across < down)), 1)
+    here = (jnp.broadcast_to(position, (slots, slots)) == across) & (far_down < row_blocks)
+    plan[0:1, :] = pick_slot(here, down, 0)
+    plan[1:2, :] = pick_slot(here, far_down, row_blocks)
+    plan[2:3, :] = pick_slot(here, column(col_list[...]) - row_blocks, 0)
+    plan[3:4, :] = tally(far_down < row_blocks, 0)
+    plan_copy = pltpu.make_async_copy(plan, plan_hbm, plan_sem)
+    plan_copy.start()
     to_smem = [
         pltpu.make_async_copy(links, link_at, link_sem.at[0]),
         pltpu.make_async_copy(last, last_at, link_sem.at[1]),
@@ -272,12 +289,12 @@
         j = at // blocks
         k = lax.rem(at, blocks)
         src_g = lax.rem(g + groups - j, groups)
-        src_b = lax.rem(b + 2 * blocks - half - k, blocks)
+        src_b = lax.rem(b + blocks - k, blocks)
 
         @pl.when((src_g != g) | (src_b != b))
         def _():
             arrived = boundary_copy(
-                j, k, lax.rem(g + j, groups), lax.rem(b + half + k, blocks), src_g * blocks + src_b
+                j, k, lax.rem(g + j, groups), lax.rem(b + k, blocks), src_g * blocks + src_b
             )
             arrived.wait_send()
             arrived.wait_recv()
@@ -286,6 +303,7 @@
 
     lax.fori_loop(0, devices, finish, 0)
     own.wait()
+    plan_copy.wait()
 
     def drain(i, _):
         out_copy(i).wait()
@@ -295,14 +313,14 @@
 
 
 def layer_kernel(
-    count_ref, row_ref, col_ref, received_hbm, partial_hbm, tiles_hbm, weight_hbm,
+    plan_ref, received_hbm, partial_hbm, tiles_hbm, weight_hbm,
     out_hbm,
-    received, tiles, weight, total, result, picked, in_sem, part_sem, tile_sem, out_sem,
+    received, tiles, weight, total, result, in_sem, part_sem, tile_sem, out_sem,
 ):
     row_blocks = total.shape[0] - 1
     per = CHUNK // TB
     chunks = row_blocks // per
-    live = count_ref[0]
+    number = plan_ref[3, 0]
 
     ins = [
         pltpu.make_async_copy(received_hbm, received, in_sem.at[0]),
@@ -313,25 +331,18 @@
         at = pl.ds(i * per, per)
         return pltpu.make_async_copy(partial_hbm.at[at], total.at[at], part_sem.at[i])
 
+    def tile_copy(n):
+        return pltpu.make_async_copy(tiles_hbm.at[plan_ref[0, n]], tiles.at[n], tile_sem.at[n])
+
+    for i in range(chunks):
+        part_copy(i).start()
     for copy in ins:
         copy.start()
 
-    def tile_copy(t, n):
-        return pltpu.make_async_copy(tiles_hbm.at[t], tiles.at[n], tile_sem.at[n])
-
-    def collect(t, n):
-        remote = col_ref[t] >= row_blocks
-
-        @pl.when(remote)
-        def _():
-            picked[n] = t
-            tile_copy(t, n).start()
-
-        return n + remote.astype(jnp.int32)
-
-    for i in range(chunks):
-        part_copy(i).start()
-    number = lax.fori_loop(0, live, collect, 0)
+    @pl.loop(0, number)
+    def _(n):
+        tile_copy(n).start()
+
     for copy in ins:
         copy.wait()
     for i in range(chunks):
@@ -344,16 +355,15 @@
 
             @pl.when(n < number)
             def _():
-                tile_copy(picked[n], n).wait()
+                tile_copy(n).wait()
 
         products = []
         places = []
         for i in range(GROUP):
             n = u * GROUP + i
-            t = picked[jnp.minimum(n, number - 1)]
-            block = received[col_ref[t] - row_blocks]
+            block = received[plan_ref[2, n]]
             products.append(jnp.dot(tiles[n], block, preferred_element_type=jnp.float32))
-            places.append(jnp.where(n < number, row_ref[t], row_blocks))
+            places.append(plan_ref[1, n])
         for product, place in zip(products, places):
             total[place] += product
 
@@ -389,14 +399,15 @@
     f32 = jnp.float32
     i32 = jnp.int32
     dma = pltpu.SemaphoreType.DMA
-    received, partial = pl.pallas_call(
+    received, partial, plan = pl.pallas_call(
         functools.partial(exchange_kernel, groups, blocks),
         out_shape=(
             jax.ShapeDtypeStruct((devices, entries, width), bf16),
             jax.ShapeDtypeStruct((chunks, CHUNK, width), f32),
+            jax.ShapeDtypeStruct((4, slots), i32),
         ),
         in_specs=[SMEM] + [ANY] * 7,
-        out_specs=(ANY, ANY),
+        out_specs=(ANY, ANY, ANY),
         scratch_shapes=[
             pltpu.VMEM((row_blocks, TB, width), bf16),
             pltpu.VMEM((1, hub_dev), i32),
@@ -418,11 +429,13 @@
             pltpu.VMEM((blocks, hub_dev, width), bf16),
             pltpu.VMEM((pairs + 1, TB, width), f32),
             pltpu.VMEM((chunks, CHUNK, width), f32),
+            pltpu.VMEM((4, slots), i32),
             dma((6,)),
             dma((4,)),
             dma((slots // PART,)),
             dma((4,)),
             dma((chunks,)),
+            dma(()),
             dma(()),
             dma((groups, blocks)),
             dma((groups, blocks)),
@@ -442,7 +455,7 @@
     out = pl.pallas_call(
         layer_kernel,
         out_shape=jax.ShapeDtypeStruct((rows, width), bf16),
-        in_specs=[SMEM, SMEM, SMEM, ANY, ANY, ANY, ANY],
+        in_specs=[SMEM, ANY, ANY, ANY, ANY],
         out_specs=ANY,
         scratch_shapes=[
             pltpu.VMEM((devices * entries // TB, TB, width), bf16),
@@ -450,7 +463,6 @@
             pltpu.VMEM(weight.shape, bf16),
             pltpu.VMEM((row_blocks + 1, TB, width), f32),
             pltpu.VMEM((rows, width), bf16),
-            pltpu.SMEM((slots,), i32),
             dma((2,)),
             dma((chunks,)),
             dma((slots,)),
@@ -459,8 +471,7 @@
         compiler_params=pltpu.CompilerParams(vmem_limit_bytes=60 << 20),
         name="layer",
     )(
-        tile_count[0], tile_row[0, 0], tile_col[0, 0],
-        received.reshape(devices * entries // TB, TB, width),
+        plan, received.reshape(devices * entries // TB, TB, width),
         partial.reshape(row_blocks, TB, width), tile_values[0, 0], weight,
     )
     return out[None, None]

time: 31.3 us -> 31 us (level)
  no operation moved by 1% of the time
where the time goes in v2:
time: 31 us; the launch traced here: 30.6 us
  Pallas kernels  29.9 us (96%)
  between operations  0.66 us (2%)
    pallas_call x1, Pallas kernels, per_device(): pl.pallas_call(functools.partial(exchange_kernel, groups, blocks), out_sh...  23.2 us
    pallas_call x1, Pallas kernels, per_device(): pl.pallas_call(layer_kernel, out_shape=jax.ShapeDtypeStruct((rows, width)...  6.72 us

profile of v2, /device:TPU:0, one launch (start us, length us, event | category | flops | bytes accessed | tf_op | source)
XLA Modules:
  0.0 30.6 jit_solution(9411284776241729795)
XLA Ops:
  0.7 23.2 %exchange.1 = (bf16[32,32,256]{2,1,0:T(8,128)(2,1)}, f32[8,512,256]{2,1,0:T(8,128)}, s32[4,160]{1,0:T(4,128)}) custom-call(s32[1]{0:T(128)} %bitcast.11.count_ref, bf16[32,128,256]{2,1,0:T(8,128)(2,1)} %bitcast.15, s32[1,32]{1,0:T(1,128)} %bitcast.21, s32[4,8,32]{2,1,0:T(8,128)} %bitcast.18, bf16[8,512,256]{2,1,0:T(8,128)(2,1)} %bitcast.16, ...), custom_call_target="tpu_custom_call" | custom-call | tf_op jit(solution)/shard_map/exchange/pallas_call | solution.py:402
  23.8 6.7 %layer.1 = bf16[4096,256]{1,0:T(8,128)(2,1)} custom-call(s32[4,160]{1,0:T(4,128)} %get-tuple-element.8.plan_ref, bf16[8,128,256]{2,1,0:T(8,128)(2,1)} %bitcast.17, f32[32,128,256]{2,1,0:T(8,128)} %bitcast.14, bf16[160,128,128]{2,1,0:T(8,128)(2,1)} %bitcast.13, bf16[256,256]{1,0:T(8,128)(2,1)} %weight_hbm.1), custom_call_target="tpu_custom_call" | custom-call | tf_op jit(solution)/shard_map/layer/pallas_call | solution.py:455
